TPU v7x, 128 devices: a whole 4x4x4 slice. The times are simulated.
128 devices in a mesh: dp: 16 (over z, x_lo, core), head: 8 (over y, x_hi).
Axes of the slice: x: 4 (x_hi: 2, x_lo: 2; x = x_hi * 2 + x_lo), y: 4, z: 4, core: 2. Of those that a mesh axis runs over, the one named last changes fastest.
Arguments:
- latents: bfloat16 [16, 1024, 3072], P('head', 'dp'), may hold values from -6 to 6
- noise: bfloat16 [16, 1024, 3072], P('head', 'dp'), may hold values from -6 to 6
- tsteps: int32 [16], replicated, may hold values from 20 to 979
- text: bfloat16 [16, 512, 3072], P('dp'), may hold values from -6 to 6
- teacher_qkv: bfloat16 [3, 3072, 3072], P(None, None, 'head'), may hold values from -3 to 3
- teacher_out: bfloat16 [3072, 3072], P('head'), may hold values from -1.5 to 1.5
- teacher_mod: bfloat16 [256, 6144], replicated, may hold values from -0.375 to 0.375
- critic_qkv: bfloat16 [3, 3072, 3072], P(None, 'dp', 'head'), may hold values from -3 to 3
- critic_out: bfloat16 [3072, 3072], P('head', 'dp'), may hold values from -1.5 to 1.5
- critic_mod: bfloat16 [256, 6144], replicated, may hold values from -0.375 to 0.375
Outputs:
- score_diff: bfloat16 [16, 1024, 3072], P('dp', 'head')
All inputs are finite; a program needn't handle non-finite values.
Results may differ from a plain program's by a relative error of at most 0.017.
Values may be sent and summed in bfloat16 or wider, within the bound.
No kernel may reach another device: no remote copies, remote signals or barrier semaphores. Data moves between devices by JAX's collectives and lax.ppermute only.
A program may use at most 192 MiB of HBM per device.

v0:
```python
import math

import jax
import jax.numpy as jnp
from jax import lax
from jax.sharding import PartitionSpec as P

HEAD_DIM = 128


def embed(tvals, width):
    half = width // 2
    freqs = jnp.exp(-math.log(10000.0) * jnp.arange(half, dtype=jnp.float32) / half)
    angle = tvals.astype(jnp.float32)[:, None] * freqs[None, :]
    return jnp.concatenate([jnp.cos(angle), jnp.sin(angle)], axis=1)


def modulate(joint, temb, w_mod):
    width = joint.shape[1]
    act = jax.nn.silu(temb).astype(jnp.bfloat16)
    mod = jnp.dot(act, w_mod, preferred_element_type=jnp.float32)
    shift = mod[:, :width]
    scale = mod[:, width:]
    rows = joint.astype(jnp.float32)
    mean = jnp.mean(rows, axis=1, keepdims=True)
    var = jnp.mean(jnp.square(rows - mean), axis=1, keepdims=True)
    norm = (rows - mean) * lax.rsqrt(var + 1e-06)
    return (norm * (1.0 + scale) + shift).astype(jnp.bfloat16)


def attend(query, keys, values, head_dim):
    heads = query.shape[1] // head_dim
    q3 = query.reshape(query.shape[0], heads, head_dim)
    k3 = keys.reshape(keys.shape[0], heads, head_dim)
    v3 = values.reshape(values.shape[0], heads, head_dim)
    scores = jnp.einsum("qhd,khd->hqk", q3, k3, preferred_element_type=jnp.float32) / math.sqrt(
        head_dim
    )
    probs = jax.nn.softmax(scores, axis=-1).astype(jnp.bfloat16)
    outs = jnp.einsum("hqk,khd->qhd", probs, v3, preferred_element_type=jnp.float32)
    return outs.astype(jnp.bfloat16).reshape(query.shape[0], heads * head_dim)


def teacher_part(joint, temb, txt, teacher_qkv, teacher_out, teacher_mod):
    hidden = modulate(joint, temb, teacher_mod)
    query = jnp.dot(hidden[txt:], teacher_qkv[0], preferred_element_type=jnp.float32).astype(
        jnp.bfloat16
    )
    keys = jnp.dot(hidden, teacher_qkv[1], preferred_element_type=jnp.float32).astype(jnp.bfloat16)
    values = jnp.dot(hidden, teacher_qkv[2], preferred_element_type=jnp.float32).astype(
        jnp.bfloat16
    )
    mixed = attend(query, keys, values, HEAD_DIM)
    return jnp.dot(mixed, teacher_out, preferred_element_type=jnp.float32)


def critic_part(joint, temb, txt, critic_qkv, critic_out, critic_mod):
    hidden = modulate(joint, temb, critic_mod)
    piece = lax.all_gather(critic_qkv, "dp", axis=1, tiled=True)
    query = jnp.dot(hidden[txt:], piece[0], preferred_element_type=jnp.float32)
    keys = jnp.dot(hidden, piece[1], preferred_element_type=jnp.float32)
    values = jnp.dot(hidden, piece[2], preferred_element_type=jnp.float32)
    mixed = attend(
        query.astype(jnp.bfloat16), keys.astype(jnp.bfloat16), values.astype(jnp.bfloat16), HEAD_DIM
    )
    return jnp.dot(
        mixed,
        lax.all_gather(critic_out, "dp", axis=1, tiled=True),
        preferred_element_type=jnp.float32,
    )


def shards(
    latents,
    noise,
    tsteps,
    text,
    teacher_qkv,
    teacher_out,
    teacher_mod,
    critic_qkv,
    critic_out,
    critic_mod,
):
    group_size = latents.shape[0]
    group = lax.axis_index("head")
    local_times = lax.dynamic_slice_in_dim(tsteps, group * group_size, group_size)
    sigma = (local_times.astype(jnp.float32) / 1000.0)[:, None, None]
    noisy = (
        (1.0 - sigma) * latents.astype(jnp.float32) + sigma * noise.astype(jnp.float32)
    ).astype(jnp.bfloat16)
    every_image = lax.all_gather(noisy, "head", axis=0, tiled=True)
    own_image = lax.all_to_all(every_image, "dp", split_axis=0, concat_axis=1, tiled=True)
    own_time = lax.dynamic_slice_in_dim(tsteps, lax.axis_index("dp"), 1)
    temb = embed(own_time, teacher_mod.shape[0])
    txt = text.shape[1]
    joint = jnp.concatenate([text[0], own_image[0]], axis=0)
    teacher_pred = teacher_part(joint, temb, txt, teacher_qkv, teacher_out, teacher_mod)
    critic_pred = critic_part(joint, temb, txt, critic_qkv, critic_out, critic_mod)
    difference = lax.psum_scatter(
        (critic_pred - teacher_pred).astype(jnp.bfloat16), "head", scatter_dimension=0, tiled=True
    )
    return difference[None]


def solution(mesh):
    in_specs = (
        P("head", "dp", None),
        P("head", "dp", None),
        P(),
        P("dp", None, None),
        P(None, None, "head"),
        P("head", None),
        P(),
        P(None, "dp", "head"),
        P("head", "dp"),
        P(),
    )
    out_specs = P("dp", "head", None)
    return jax.shard_map(shards, mesh=mesh, in_specs=in_specs, out_specs=out_specs, check_vma=False)
```

profile of v0, /device:TPU:4, one launch (start us, length us, event | category | flops | bytes accessed | tf_op | source)
XLA Modules:
  0.0 462.4 jit_solution(17158986421504169671)
XLA Ops:
  6.5 0.9 broadcast_subtract_fusion
  7.4 2.7 add_convert_fusion
  10.9 88.1 %all-gather.4.cloned.1.call-done = bf16[16,64,3072]{2,1,0:T(8,128)(2,1)} async-done(((bf16[2,64,3072]{2,1,0:T(8,128)(2,1)}), bf16[16,64,3072]{2,1,0:T(8,128)(2,1)}) %all-gather.4.cloned.1.call-update) | async-done | bytes 6291472 | tf_op jit(solution)/shard_map/all_gather | solution.py:92
  99.0 6.1 %all-to-all-start = ((bf16[16,64,3072]{2,1,0:T(8,128)(2,1)}), bf16[16,64,3072]{2,1,0:T(8,128)(2,1)}, u32[]{:S(2)}, u32[]{:S(2)}) async-start(bf16[16,64,3072]{2,1,0:T(8,128)(2,1)} %all-gather.4.cloned.1.call-done), calls=%async_computation | async-start | bytes 12582912 | tf_op jit(solution)/shard_map/all_to_all | solution.py:93
  107.7 2.6 fusion.66
  110.3 110.9 %all-to-all-done = bf16[16,64,3072]{2,1,0:T(8,128)(2,1)} async-done(((bf16[16,64,3072]{2,1,0:T(8,128)(2,1)}), bf16[16,64,3072]{2,1,0:T(8,128)(2,1)}, u32[]{:S(2)}, u32[]{:S(2)}) %all-to-all-start) | async-done | bytes 6291488 | tf_op jit(solution)/shard_map/all_to_all | solution.py:93
  221.2 5.0 %convert_reduce_fusion = f32[1536]{0:T(1024)S(1)} fusion(bf16[1024,3072]{1,0:T(8,128)(2,1)} %bitcast.1, bf16[512,3072]{1,0:T(8,128)(2,1)} %bitcast.70), kind=kLoop, calls=%fused_computation.3 | loop fusion | flops 23591424 | bytes 9443328 | tf_op jit(solution)/shard_map/reduce_sum | solution.py:25
  226.3 6.7 %fusion.10 = f32[1536]{0:T(1024)S(1)} fusion(f32[1536]{0:T(1024)S(1)} %broadcast_multiply_fusion, bf16[1024,3072]{1,0:T(8,128)(2,1)} %bitcast.1, bf16[512,3072]{1,0:T(8,128)(2,1)S(1)} %bitcast.71), kind=kLoop, calls=%fused_computation.12 | loop fusion | flops 33028608 | bytes 9449472 | tf_op jit(solution)/shard_map/reduce_sum | solution.py:26
  233.0 14.9 %fusion.9 = (bf16[1536,3072]{1,0:T(8,128)(2,1)}, bf16[1536,3072]{1,0:T(8,128)(2,1)}) fusion(f32[3072]{0:T(1024)S(1)} %bitcast.86, f32[3072]{0:T(1024)S(1)} %bitcast.85, f32[1536]{0:T(1024)S(1)} %add_rsqrt_fusion, f32[1536]{0:T(1024)S(1)} %broadcast_multiply_fusion, bf16[1024,3072]{1,0:T(8,128)(2,1)} %bitcast.1, bf16[512,3072]{1,0:T(8,128)(2,1)S(1)} %bitcast.72, ...), kind=kLoop, calls=%fused_computation.11 | loop fusion | flops 56623104 | bytes 28372992 | tf_op jit(solution)/shard_map/convert_element_type | solution.py:28
  247.9 6.4 %fusion.33 = bf16[1024,384]{0,1:T(8,128)(2,1)S(1)} fusion(bf16[3,3072,384]{2,1,0:T(8,128)(2,1)} %all-gather.6.cloned.1.call-done, bf16[1536,3072]{1,0:T(8,128)(2,1)} %get-tuple-element.8), kind=kOutput, calls=%fused_computation.47 | convolution fusion | flops 2416312320 | bytes 9437184 | tf_op jit(solution)/shard_map/dot_general | solution.py:60
  254.3 5.7 %convolution_convert_fusion.2 = bf16[1536,384]{0,1:T(8,128)(2,1)S(1)} fusion(bf16[1536,3072]{1,0:T(8,128)(2,1)S(1)} %copy-done.3, bf16[3,3072,384]{2,1,0:T(8,128)(2,1)} %all-gather.6.cloned.1.call-done), kind=kOutput, calls=%fused_computation.33 | convolution fusion | flops 3624468480 | bytes 12976128 | tf_op jit(solution)/shard_map/dot_general | solution.py:61
  259.9 6.7 %fusion.64 = f32[3,1024]{1,0:T(4,128)S(1)} fusion(bf16[1024,3,128]{0,2,1:T(8,128)(2,1)S(1)} %bitcast.80, bf16[1536,3,128]{0,2,1:T(8,128)(2,1)S(1)} %bitcast.78), kind=kOutput, calls=%fused_computation.69 | convolution fusion | flops 1222116864 | bytes 1978368 | tf_op jit(solution)/shard_map/sub | solution.py:39
  266.7 8.6 %fusion.67 = f32[3,1024,1536]{2,1,0:T(8,128)} fusion(bf16[1024,3,128]{0,2,1:T(8,128)(2,1)S(1)} %bitcast.81, bf16[1536,3,128]{0,2,1:T(8,128)(2,1)S(1)} %bitcast.79), kind=kOutput, calls=%fused_computation.72 | convolution fusion | flops 1207959552 | bytes 20840448 | tf_op jit(solution)/shard_map/qhd,khd->hqk/dot_general | solution.py:36
  275.3 8.3 %convolution_convert_fusion = bf16[1536,384]{0,1:T(8,128)(2,1)S(1)} fusion(bf16[1536,3072]{1,0:T(8,128)(2,1)} %get-tuple-element.7, bf16[3,3072,384]{2,1,0:T(8,128)(2,1)} %param.14), kind=kOutput, calls=%fused_computation.31 | convolution fusion | flops 3624468480 | bytes 12976128 | tf_op jit(solution)/shard_map/dot_general | solution.py:49
  283.6 6.7 %convolution_convert_fusion.3 = bf16[1536,384]{0,1:T(8,128)(2,1)} fusion(bf16[1536,3072]{1,0:T(8,128)(2,1)S(1)} %bitcast.74, bf16[3,3072,384]{2,1,0:T(8,128)(2,1)} %all-gather.6.cloned.1.call-done), kind=kOutput, calls=%fused_computation.34 | convolution fusion | flops 3624468480 | bytes 12976128 | tf_op jit(solution)/shard_map/dot_general | solution.py:62
  290.4 15.8 %fusion.32 = bf16[3,128,1024]{2,1,0:T(8,128)(2,1)S(1)} fusion(bf16[1536,3,128]{0,2,1:T(8,128)(2,1)} %bitcast.89, f32[3,1024]{1,0:T(4,128)S(1)} %fusion.64, f32[3,1024,1536]{2,1,0:T(8,128)} %fusion.67), kind=kOutput, calls=%fused_computation.46 | convolution fusion | flops 1231950336 | bytes 20852736 | tf_op jit(solution)/shard_map/hqk,khd->qhd/dot_general | solution.py:40
  306.1 6.1 %fusion.36 = bf16[1024,384]{0,1:T(8,128)(2,1)S(1)} fusion(bf16[3,3072,384]{2,1,0:T(8,128)(2,1)} %param.14, bf16[1536,3072]{1,0:T(8,128)(2,1)} %get-tuple-element.7), kind=kOutput, calls=%fused_computation.48 | convolution fusion | flops 2416312320 | bytes 9437184 | tf_op jit(solution)/shard_map/dot_general | solution.py:46
  312.3 6.6 %fusion.65 = f32[3,1024]{1,0:T(4,128)S(1)} fusion(bf16[1024,3,128]{0,2,1:T(8,128)(2,1)S(1)} %bitcast.82, bf16[1536,3,128]{0,2,1:T(8,128)(2,1)S(1)} %bitcast.76), kind=kOutput, calls=%fused_computation.70 | convolution fusion | flops 1222116864 | bytes 1978368 | tf_op jit(solution)/shard_map/sub | solution.py:39
  318.8 8.0 %fusion.70 = f32[3,1024,1536]{2,1,0:T(8,128)} fusion(bf16[1024,3,128]{0,2,1:T(8,128)(2,1)S(1)} %bitcast.83, bf16[1536,3,128]{0,2,1:T(8,128)(2,1)S(1)} %bitcast.77), kind=kOutput, calls=%fused_computation.75 | convolution fusion | flops 1207959552 | bytes 20840448 | tf_op jit(solution)/shard_map/qhd,khd->hqk/dot_general | solution.py:36
  326.9 8.2 %convolution_convert_fusion.1 = bf16[1536,384]{0,1:T(8,128)(2,1)S(1)} fusion(bf16[1536,3072]{1,0:T(8,128)(2,1)} %get-tuple-element.7, bf16[3,3072,384]{2,1,0:T(8,128)(2,1)} %param.14), kind=kOutput, calls=%fused_computation.32 | convolution fusion | flops 3624468480 | bytes 12976128 | tf_op jit(solution)/shard_map/dot_general | solution.py:50
  335.1 15.9 %fusion.31 = bf16[3,128,1024]{2,1,0:T(8,128)(2,1)} fusion(bf16[1536,3,128]{0,2,1:T(8,128)(2,1)S(1)} %bitcast.90, f32[3,1024]{1,0:T(4,128)S(1)} %fusion.65, f32[3,1024,1536]{2,1,0:T(8,128)} %fusion.70), kind=kOutput, calls=%fused_computation.45 | convolution fusion | flops 1231950336 | bytes 20852736 | tf_op jit(solution)/shard_map/hqk,khd->qhd/dot_general | solution.py:40
  351.1 5.3 %fusion.68 = f32[1024,3072]{1,0:T(8,128)S(1)} fusion(bf16[1024,384]{0,1:T(8,128)(2,1)S(1)} %bitcast.84, bf16[384,3072]{0,1:T(8,128)(2,1)} %all-gather.8.cloned.1.call-done), kind=kOutput, calls=%fused_computation.73 | convolution fusion | flops 2415919104 | bytes 15728640 | tf_op jit(solution)/shard_map/dot_general | solution.py:66
  356.4 5.6 %subtract_convert_fusion = bf16[1024,3072]{1,0:T(8,128)(2,1)} fusion(f32[1024,3072]{1,0:T(8,128)S(1)} %fusion.68, bf16[1024,384]{0,1:T(8,128)(2,1)S(1)} %bitcast.75, bf16[384,3072]{1,0:T(8,128)(2,1)S(1)} %copy-done.5), kind=kOutput, calls=%fused_computation.21 | convolution fusion | flops 2422210560 | bytes 22020096 | tf_op jit(solution)/shard_map/dot_general | solution.py:54
  362.0 93.6 %reduce-scatter.2.cloned.1.call-done = bf16[128,3072]{1,0:T(8,128)(2,1)} async-done(((bf16[1024,3072]{1,0:T(8,128)(2,1)}), bf16[128,3072]{1,0:T(8,128)(2,1)}) %reduce-scatter.2.cloned.1.call-update) | async-done | bytes 786448 | tf_op jit(solution)/shard_map/reduce_scatter | solution.py:100
  (40 shorter events, 2.8 us)
Async XLA Ops:
  6.5 100.7 %copy-start = (bf16[256,6144]{1,0:T(8,128)(2,1)S(1)}, bf16[256,6144]{1,0:T(8,128)(2,1)}, u32[]{:S(2)}) copy-start(bf16[256,6144]{1,0:T(8,128)(2,1)} %param.16) | copy-start | bytes 9437188
  6.5 99.3 %copy-start.6 = (s32[16]{0:T(128)S(1)}, s32[16]{0:T(128)}, u32[]{:S(2)}) copy-start(s32[16]{0:T(128)} %param.12) | copy-start | bytes 196
  6.5 92.4 %all-gather.4.cloned.1.call-start = ((), (), s32[]{:S(2)}) async-start(), calls=%async_computation.2 | async-start | bytes 7077888 | tf_op jit(solution)/shard_map/all_gather | solution.py:92
  10.1 237.8 %all-gather.6.cloned.1.call-start = ((), (), s32[]{:S(2)}) async-start(), calls=%async_computation.3 | async-start | bytes 7520256 | tf_op jit(solution)/shard_map/all_gather | solution.py:59
  99.0 122.2 %all-to-all-start = ((bf16[16,64,3072]{2,1,0:T(8,128)(2,1)}), bf16[16,64,3072]{2,1,0:T(8,128)(2,1)}, u32[]{:S(2)}, u32[]{:S(2)}) async-start(bf16[16,64,3072]{2,1,0:T(8,128)(2,1)} %all-gather.4.cloned.1.call-done), calls=%async_computation | async-start | bytes 12582912 | tf_op jit(solution)/shard_map/all_to_all | solution.py:93
  105.1 246.0 %all-gather.8.cloned.1.call-start = ((), (), s32[]{:S(2)}) async-start(), calls=%async_computation.4 | async-start | bytes 2506752 | tf_op jit(solution)/shard_map/all_gather | solution.py:68
  105.8 349.7 %reduce-scatter.2.cloned.1.call-start = ((), (), s32[]{:S(2)}) async-start(), calls=%async_computation.5 | async-start | bytes 7077888 | tf_op jit(solution)/shard_map/reduce_scatter | solution.py:100
  107.7 118.5 %copy-start.2 = (bf16[1,512,3072]{2,1,0:T(8,128)(2,1)S(1)}, bf16[1,512,3072]{2,1,0:T(8,128)(2,1)}, u32[]{:S(2)}) copy-start(bf16[1,512,3072]{2,1,0:T(8,128)(2,1)} %param.13) | copy-start | bytes 9437188
  247.9 6.4 %copy-start.3 = (bf16[1536,3072]{1,0:T(8,128)(2,1)S(1)}, bf16[1536,3072]{1,0:T(8,128)(2,1)}, u32[]{:S(2)}) copy-start(bf16[1536,3072]{1,0:T(8,128)(2,1)} %get-tuple-element.8) | copy-start | bytes 28311556
  266.7 16.9 %slice-start = ((s8[9437184]{0:T(1024)(128)(4,1)}), s8[4194304]{0:T(1024)(128)(4,1)S(1)}, s32[]{:S(2)}) async-start(s8[9437184]{0:T(1024)(128)(4,1)} %bitcast.73), calls=%async_computation.6 | async-start | bytes 8388608
  266.7 16.9 %slice-start.1 = ((s8[9437184]{0:T(1024)(128)(4,1)}), s8[4194304]{0:T(1024)(128)(4,1)S(1)}, s32[]{:S(2)}) async-start(s8[9437184]{0:T(1024)(128)(4,1)} %bitcast.73), calls=%async_computation.7 | async-start | bytes 8388608
  275.3 8.3 %slice-start.2 = ((s8[9437184]{0:T(1024)(128)(4,1)}), s8[1048576]{0:T(1024)(128)(4,1)S(1)}, s32[]{:S(2)}) async-start(s8[9437184]{0:T(1024)(128)(4,1)} %bitcast.73), calls=%async_computation.8 | async-start | bytes 2097152
  351.0 5.3 %copy-start.4 = (bf16[3,128,1024]{2,1,0:T(8,128)(2,1)S(1)}, bf16[3,128,1024]{2,1,0:T(8,128)(2,1)}, u32[]{:S(2)}) copy-start(bf16[3,128,1024]{2,1,0:T(8,128)(2,1)} %fusion.31) | copy-start | bytes 2359300
  351.0 5.3 %copy-start.5 = (bf16[384,3072]{1,0:T(8,128)(2,1)S(1)}, bf16[384,3072]{1,0:T(8,128)(2,1)}, u32[]{:S(2)}) copy-start(bf16[384,3072]{1,0:T(8,128)(2,1)} %param.15) | copy-start | bytes 7077892
  356.4 99.2 %copy-start.1 = (bf16[256,6144]{1,0:T(8,128)(2,1)S(1)}, bf16[256,6144]{1,0:T(8,128)(2,1)}, u32[]{:S(2)}) copy-start(bf16[256,6144]{1,0:T(8,128)(2,1)} %param.16) | copy-start | bytes 9437188
Sparse Core Ops, SparseCore 0:
  10.2 88.6 all-gather.3
  100.6 115.5 all-gather.5
  217.9 35.9 all-gather.7
  362.1 93.3 reduce-scatter.1
where the time goes:
time: 468 us; the launch traced here: 462 us
  waiting for transfers between devices  294 us (63%)
  matrix products  117 us (25%)
  other arithmetic  30.3 us (6%)
  between operations  14.3 us (3%)
  starting transfers between devices  6.21 us (1%)
    all_to_all x1, waiting for transfers between devices, shards(): lax.all_to_all(every_image, 'dp', split_axis=0, concat_axis=1, tiled=True)  111 us
    reduce_scatter x1, waiting for transfers between devices, shards(): lax.psum_scatter((critic_pred - teacher_pred).astype(jnp.bfloat16), 'head...  93.6 us
    all_gather x1, waiting for transfers between devices, shards(): every_image = lax.all_gather(noisy, 'head', axis=0, tiled=True)  88.1 us
    dot_general x2, matrix products, attend(): jnp.einsum('hqk,khd->qhd', probs, v3, preferred_element_type=jnp.float32)  31.7 us
    dot_general x2, matrix products, attend(): jnp.einsum('qhd,khd->hqk', q3, k3, preferred_element_type=jnp.float32)  16.6 us
    convert_element_type x1, other arithmetic, modulate(): return (norm * (1.0 + scale) + shift).astype(jnp.bfloat16)  14.9 us
    sub x2, matrix products, attend(): probs = jax.nn.softmax(scores, axis=-1).astype(jnp.bfloat16)  13.3 us
  transfers between devices with their start and end apart: 5, of which 3 were waited for; matrix products, arithmetic and copies ran while one was open for 29% of the time, Pallas kernels for 0%

commit v1 on v0

v1 whole, which is shorter than its diff:
```python
import functools
import math

import jax
import jax.numpy as jnp
from jax import lax
from jax.experimental import pallas as pl
from jax.experimental.pallas import tpu as pltpu
from jax.sharding import PartitionSpec as P

HEAD_DIM = 128
BLOCK = 128
HALF = 64
F32 = jnp.float32
BF16 = jnp.bfloat16
MIB = 1 << 20


def embed(tvals, width):
    half = width // 2
    freqs = jnp.exp(-math.log(10000.0) * jnp.arange(half, dtype=F32) / half)
    angle = tvals.astype(F32)[:, None] * freqs[None, :]
    return jnp.concatenate([jnp.cos(angle), jnp.sin(angle)], axis=1)


def modulation(temb, w_mod):
    act = jax.nn.silu(temb).astype(BF16)
    mod = jnp.dot(act, w_mod, preferred_element_type=F32)
    return mod.reshape(2, w_mod.shape[1] // 2)


def project_kernel(sizes, chunk, *refs):
    xs, (mod_ref, w_ref, o_ref, h_ref) = refs[: len(sizes)], refs[len(sizes) :]

    @pl.when(pl.program_id(0) == 0)
    def _():
        shift = mod_ref[0:1, :]
        gain = 1.0 + mod_ref[1:2, :]
        base = 0
        for x_ref, size in zip(xs, sizes):

            def step(i, _, x_ref=x_ref, base=base):
                start = pl.multiple_of(i * chunk, chunk)
                rows = x_ref[pl.ds(start, chunk), :].astype(F32)
                mean = jnp.mean(rows, axis=1, keepdims=True)
                rows = rows - mean
                var = jnp.mean(rows * rows, axis=1, keepdims=True)
                norm = rows * lax.rsqrt(var + 1e-06)
                h_ref[pl.ds(pl.multiple_of(base + start, chunk), chunk), :] = (
                    norm * gain + shift
                ).astype(BF16)
                return 0

            lax.fori_loop(0, size // chunk, step, 0)
            base += size

    o_ref[0] = jnp.dot(h_ref[...], w_ref[0], preferred_element_type=F32).astype(BF16)


def project(blocks, mod, weights, first):
    sizes = [b.shape[0] for b in blocks]
    rows, width = sum(sizes), blocks[0].shape[1]
    count, columns = weights.shape[0] - first, weights.shape[2]
    whole = [pl.BlockSpec(b.shape, lambda j: (0, 0)) for b in blocks]
    return pl.pallas_call(
        functools.partial(project_kernel, sizes, 16),
        out_shape=jax.ShapeDtypeStruct((count, rows, columns), BF16),
        grid=(count,),
        in_specs=whole
        + [
            pl.BlockSpec((2, width), lambda j: (0, 0)),
            pl.BlockSpec((1, width, columns), lambda j: (j + first, 0, 0)),
        ],
        out_specs=pl.BlockSpec((1, rows, columns), lambda j: (j, 0, 0)),
        scratch_shapes=[pltpu.VMEM((rows, width), BF16)],
        compiler_params=pltpu.CompilerParams(vmem_limit_bytes=40 * MIB),
        cost_estimate=pl.CostEstimate(
            flops=2 * rows * width * columns * count,
            bytes_accessed=2 * (rows * width + count * width * columns),
            transcendentals=0,
        ),
        name="project",
    )(*blocks, mod, weights)


def attend_kernel(places, groups, *refs):
    critic, teacher = refs[:groups], refs[groups : 2 * groups]
    wc_ref, wt_ref = refs[2 * groups : 2 * groups + 2]
    outs = refs[2 * groups + 2 : -1]
    o_ref = refs[-1]
    columns = wc_ref.shape[0]
    factor = math.log2(math.e) / math.sqrt(HEAD_DIM)
    for m, model in enumerate((critic, teacher)):
        for head in range(columns // HEAD_DIM):
            at = pl.ds(head * HEAD_DIM, HEAD_DIM)
            query = jnp.concatenate(
                [model[g][0, pl.ds(row, BLOCK), at] for g, row in places], axis=0
            )
            scores = [
                lax.dot_general(
                    query,
                    ref[ref.shape[0] - 2, :, at],
                    (((1,), (1,)), ((), ())),
                    preferred_element_type=F32,
                )
                for ref in model
            ]
            top = functools.reduce(
                jnp.maximum, [jnp.max(s, axis=1, keepdims=True) for s in scores]
            )
            total = 0.0
            mixed = 0.0
            for s, ref in zip(scores, model):
                prob = jnp.exp2((s - top) * factor)
                total = total + jnp.sum(prob, axis=1, keepdims=True)
                mixed = mixed + jnp.dot(
                    prob.astype(BF16),
                    ref[ref.shape[0] - 1, :, at],
                    preferred_element_type=F32,
                )
            o_ref[:, pl.ds(m * columns + head * HEAD_DIM, HEAD_DIM)] = (
                mixed / total
            ).astype(BF16)
    width = wc_ref.shape[1]
    part = width // 4
    for j in range(4):
        at = pl.ds(j * part, part)
        diff = jnp.dot(
            o_ref[:, :columns], wc_ref[:, at], preferred_element_type=F32
        ) - jnp.dot(o_ref[:, columns:], wt_ref[:, at], preferred_element_type=F32)
        for i, out in enumerate(outs):
            out[:, at] = diff[i * HALF : (i + 1) * HALF].astype(out.dtype)


def attend(places, critic, teacher, wc, wt):
    rows = BLOCK * len(places)
    columns, width = wc.shape
    keys = sum(g.shape[1] for g in critic)
    return pl.pallas_call(
        functools.partial(attend_kernel, places, len(critic)),
        out_shape=[jax.ShapeDtypeStruct((HALF, width), BF16)] * (rows // HALF),
        scratch_shapes=[pltpu.VMEM((rows, 2 * columns), BF16)],
        compiler_params=pltpu.CompilerParams(vmem_limit_bytes=48 * MIB),
        cost_estimate=pl.CostEstimate(
            flops=8 * rows * columns * (2 * keys + width),
            bytes_accessed=2 * (6 * keys * columns + 2 * columns * width + rows * width),
            transcendentals=6 * rows * keys,
        ),
        name="attend",
    )(*critic, *teacher, wc, wt)


def shards(
    latents,
    noise,
    tsteps,
    text,
    teacher_qkv,
    teacher_out,
    teacher_mod,
    critic_qkv,
    critic_out,
    critic_mod,
):
    images = latents.shape[0]
    n_dp, n_head = lax.axis_size("dp"), lax.axis_size("head")
    dp, head = lax.axis_index("dp"), lax.axis_index("head")
    core = dp % 2

    wc_qkv = lax.all_gather(critic_qkv, "dp", axis=1, tiled=True)
    wc_out = lax.all_gather(critic_out, "dp", axis=1, tiled=True)

    local_times = lax.dynamic_slice_in_dim(tsteps, head * images, images)
    sigma = (local_times.astype(F32) / 1000.0)[:, None, None]
    noisy = ((1.0 - sigma) * latents.astype(F32) + sigma * noise.astype(F32)).astype(BF16)

    def cross(flip):
        return [
            (d * n_head + h, (2 * h + (d % 2) ^ flip) * n_head + d // 2)
            for d in range(n_dp)
            for h in range(n_head)
        ]

    first = jnp.where(core == 0, noisy[0], noisy[1])
    second = jnp.where(core == 0, noisy[1], noisy[0])
    own = jnp.concatenate(
        [
            lax.ppermute(first, ("dp", "head"), cross(0)),
            lax.ppermute(second, ("dp", "head"), cross(1)),
        ],
        axis=0,
    )

    up = [(i, (i + 2) % n_head) for i in range(n_head)]
    down = [(i, (i - 2) % n_head) for i in range(n_head)]
    swap = [(i, i ^ 1) for i in range(n_head)]

    def go(x, perm):
        return lax.ppermute(x, "head", perm)

    own_below, own_above = go(own, up), go(own, down)
    other = go(own, swap)
    far_a, far_b = go(own_below[:HALF], up), go(own_above[HALF:], down)
    other_below, other_above = go(other, up), go(other, down)
    other_far_a = go(other_below[:HALF], up)
    other_far_b = go(other_above[HALF:], down)

    own_time = lax.dynamic_slice_in_dim(tsteps, dp, 1)
    temb = embed(own_time, teacher_mod.shape[0])
    arrivals = [
        [own, own_below, own_above, other],
        [far_a, far_b, other_below, other_above],
        [other_far_a, other_far_b],
    ]

    def keyed(w, w_mod):
        mod = modulation(temb, w_mod)
        return [project([text[0]], mod, w, 1)] + [project(a, mod, w, 0) for a in arrivals]

    teacher = keyed(teacher_qkv, teacher_mod)
    critic = keyed(wc_qkv, critic_mod)

    far = [(3, 0), (2, 0)]
    near_other = [(2, BLOCK), (2, 2 * BLOCK)]
    near_own = [(1, BLOCK), (1, 2 * BLOCK)]
    here = [(1, 3 * BLOCK), (1, 0)]

    def run(places):
        return attend(places, critic, teacher, wc_out, teacher_out)

    def add(*parts):
        return functools.reduce(jnp.add, [p.astype(F32) for p in parts]).astype(BF16)

    fo_a, fo_b, f_a, f_b = run(far)
    via_o_a, via_o_b = go(fo_a, up), go(fo_b, down)
    via_a, via_b = go(f_a, up), go(f_b, down)
    ob_a, ob_b, oa_a, oa_b = run(near_other)
    so_below_a, so_above_b = go(ob_a, down), go(oa_b, up)
    so_below_b, so_above_a = go(add(ob_b, via_o_b), down), go(add(oa_a, via_o_a), up)
    nb_a, nb_b, na_a, na_b = run(near_own)
    s_below_a, s_above_b = go(nb_a, down), go(na_b, up)
    s_below_b, s_above_a = go(add(nb_b, via_b), down), go(add(na_a, via_a), up)
    ho_a, ho_b, h_a, h_b = run(here)
    cross_a = go(add(ho_a, so_below_a, so_above_a), swap)
    cross_b = go(add(ho_b, so_below_b, so_above_b), swap)
    top = add(h_a, s_below_a, s_above_a, cross_a)
    low = add(h_b, s_below_b, s_above_b, cross_b)
    out = jnp.where(
        core == 0,
        jnp.concatenate([top, low], axis=0),
        jnp.concatenate([low, top], axis=0),
    )
    return out[None]


def solution(mesh):
    in_specs = (
        P("head", "dp", None),
        P("head", "dp", None),
        P(),
        P("dp", None, None),
        P(None, None, "head"),
        P("head", None),
        P(),
        P(None, "dp", "head"),
        P("head", "dp"),
        P(),
    )
    out_specs = P("dp", "head", None)
    return jax.shard_map(shards, mesh=mesh, in_specs=in_specs, out_specs=out_specs, check_vma=False)
```

time: 468 us -> 305 us (0.65)
  waiting for transfers between devices: 294 us -> 62.7 us
  Pallas kernels: 0 us -> 116 us
  matrix products: 117 us -> 5.36 us
  starting transfers between devices: 6.21 us -> 80.2 us
  other arithmetic: 30.3 us -> 4.82 us
  local copies, waits for them, and re-layouts: 0.63 us -> 16.2 us
    pallas_call x0 -> x12, Pallas kernels: none -> 116 us  [the longest x8 80 us: project(): pl.pallas_call(functools.partial(project_kernel, sizes, 16), out_shape=ja...]
    all_to_all x1 -> x0, waiting for transfers between devices: 111 us -> none  [shards(): lax.all_to_all(every_image, 'dp', split_axis=0, concat_axis=1, tiled=True)]
    dot_general x14 -> x2, matrix products: 104 us -> 5.36 us  [modulation(): mod = jnp.dot(act, w_mod, preferred_element_type=F32)]
    reduce_scatter x1 -> x0, waiting for transfers between devices: 93.6 us -> none  [shards(): lax.psum_scatter((critic_pred - teacher_pred).astype(jnp.bfloat16), 'head...]
    all_gather x3 -> x2, waiting for transfers between devices: 88.1 us -> 0.01 us  [the longest x1 0.01 us: shards(): wc_out = lax.all_gather(critic_out, 'dp', axis=1, tiled=True)]
    ppermute x0 -> x25, starting transfers between devices: none -> 80.1 us  [the longest x23 77 us: go(): return lax.ppermute(x, 'head', perm)]
    ppermute x0 -> x25, waiting for transfers between devices: none -> 61.3 us  [the longest x23 45.2 us: go(): return lax.ppermute(x, 'head', perm)]
    convert_element_type x3 -> x8, other arithmetic: 17.6 us -> 2.54 us  [the longest x1 1.86 us: shards(): ((1.0 - sigma) * latents.astype(F32) + sigma * noise.astype(F32)).astype(...]
  transfers between devices with their start and end apart: 5 -> 27, of which waited for: 3 -> 9; matrix products, arithmetic and copies ran while one was open for 29% -> 5% of each run, Pallas kernels for 0% -> 16%
where the time goes in v1:
time: 305 us; the launch traced here: 300 us
  Pallas kernels  116 us (38%)
  starting transfers between devices  80.2 us (26%)
  waiting for transfers between devices  62.7 us (21%)
  local copies, waits for them, and re-layouts  16.2 us (5%)
  between operations  15.1 us (5%)
  matrix products  5.36 us (2%)
  other arithmetic  4.82 us (2%)
    pallas_call x8, Pallas kernels, project(): pl.pallas_call(functools.partial(project_kernel, sizes, 16), out_shape=ja...  80 us
    ppermute x23, starting transfers between devices, go(): return lax.ppermute(x, 'head', perm)  77 us
    ppermute x23, waiting for transfers between devices, go(): return lax.ppermute(x, 'head', perm)  45.2 us
    pallas_call x4, Pallas kernels, attend(): pl.pallas_call(functools.partial(attend_kernel, places, len(critic)), out...  35.7 us
    ppermute x1, waiting for transfers between devices, shards(): lax.ppermute(first, ('dp', 'head'), cross(0))  10.7 us
    unnamed x61, local copies, waits for them, and re-layouts  10.3 us
  transfers between devices with their start and end apart: 27, of which 9 were waited for; matrix products, arithmetic and copies ran while one was open for 5% of the time, Pallas kernels for 16%

profile of v1, /device:TPU:4, one launch (start us, length us, event | category | flops | bytes accessed | tf_op | source)
XLA Modules:
  0.0 300.1 jit_solution(534362963557023537)
XLA Ops:
  13.9 10.7 %collective-permute-done = bf16[64,3072]{1,0:T(8,128)(2,1)S(1)} collective-permute-done((bf16[64,3072]{1,0:T(8,128)(2,1)S(1)}, bf16[64,3072]{1,0:T(8,128)(2,1)S(1)}, u32[]{:S(2)}, u32[]{:S(2)}) %collective-permute-start) | collective-permute-done | bytes 393248 | tf_op jit(solution)/shard_map/ppermute | solution.py:188
  25.4 5.4 %collective-permute-done.1 = bf16[64,3072]{1,0:T(8,128)(2,1)S(1)} collective-permute-done((bf16[64,3072]{1,0:T(8,128)(2,1)S(1)}, bf16[64,3072]{1,0:T(8,128)(2,1)S(1)}, u32[]{:S(2)}, u32[]{:S(2)}) %collective-permute-start.1) | collective-permute-done | bytes 393248 | tf_op jit(solution)/shard_map/ppermute | solution.py:189
  32.8 19.5 %collective-permute-start.2 = (bf16[128,3072]{1,0:T(8,128)(2,1)}, bf16[128,3072]{1,0:T(8,128)(2,1)S(1)}, u32[]{:S(2)}, u32[]{:S(2)}) collective-permute-start(bf16[128,3072]{1,0:T(8,128)(2,1)} %constant_dynamic-update-slice_fusion.refs_0_), channel_id=1, source_target_pairs={{0,2},{1,3},{2,4},{3,5},{4,6},{5,7},{6,0},{7,1},{8,10},{9,11},{10,... | collective-permute-start | bytes 2359304 | tf_op jit(solution)/shard_map/ppermute | solution.py:199
  52.4 4.7 %collective-permute-start.3 = (bf16[128,3072]{1,0:T(8,128)(2,1)}, bf16[128,3072]{1,0:T(8,128)(2,1)S(1)}, u32[]{:S(2)}, u32[]{:S(2)}) collective-permute-start(bf16[128,3072]{1,0:T(8,128)(2,1)} %constant_dynamic-update-slice_fusion.refs_0_), channel_id=1, source_target_pairs={{0,6},{1,7},{2,0},{3,1},{4,2},{5,3},{6,4},{7,5},{8,14},{9,15},{10,... | collective-permute-start | bytes 2359304 | tf_op jit(solution)/shard_map/ppermute | solution.py:199
  57.2 21.0 %collective-permute-start.7 = (bf16[128,3072]{1,0:T(8,128)(2,1)}, bf16[128,3072]{1,0:T(8,128)(2,1)S(1)}, u32[]{:S(2)}, u32[]{:S(2)}) collective-permute-start(bf16[128,3072]{1,0:T(8,128)(2,1)} %collective-permute-done.4.refs_3_), channel_id=1, source_target_pairs={{0,2},{1,3},{2,4},{3,5},{4,6},{5,7},{6,0},{7,1},{8,10},{9,11},{10,... | collective-permute-start | bytes 2359304 | tf_op jit(solution)/shard_map/ppermute | solution.py:199
  78.2 6.0 %collective-permute-start.8 = (bf16[128,3072]{1,0:T(8,128)(2,1)}, bf16[128,3072]{1,0:T(8,128)(2,1)S(1)}, u32[]{:S(2)}, u32[]{:S(2)}) collective-permute-start(bf16[128,3072]{1,0:T(8,128)(2,1)} %collective-permute-done.4.refs_3_), channel_id=1, source_target_pairs={{0,6},{1,7},{2,0},{3,1},{4,2},{5,3},{6,4},{7,5},{8,14},{9,15},{10,... | collective-permute-start | bytes 2359304 | tf_op jit(solution)/shard_map/ppermute | solution.py:199
  93.0 11.5 %project.12.refs_4_ = bf16[2,512,384]{2,1,0:T(8,128)(2,1)S(1)} custom-call(bf16[512,3072]{1,0:T(8,128)(2,1)S(1)} %bitcast.32, f32[2,3072]{1,0:T(2,128)S(1)} %bitcast.38, bf16[3,3072,384]{2,1,0:T(8,128)(2,1)S(1)} %bitcast.29), custom_call_target="tpu_custom_call" | custom-call | flops 2415919104 | bytes 7864320 | tf_op jit(solution)/shard_map/project/pallas_call | solution.py:65
  107.0 14.6 %project.13.refs_5_ = bf16[3,512,384]{2,1,0:T(8,128)(2,1)S(1)} custom-call(bf16[128,3072]{1,0:T(8,128)(2,1)} %constant_dynamic-update-slice_fusion.refs_0_, bf16[128,3072]{1,0:T(8,128)(2,1)S(1)} %collective-permute-done.2.refs_1_, bf16[128,3072]{1,0:T(8,128)(2,1)S(1)} %collective-permute-done.3.refs_2_, bf16[128,3072]{1,0:T(8,128)(2,1)} %collective-permute-done.4.refs_3_, ...), custom_call_target="tpu_custom_call" | custom-call | flops 3623878656 | bytes 10223616 | tf_op jit(solution)/shard_map/project/pallas_call | solution.py:65
  122.7 10.0 %project.14.refs_6_ = bf16[3,384,384]{2,1,0:T(8,128)(2,1)S(1)} custom-call(bf16[64,3072]{1,0:T(8,128)(2,1)S(1)} %collective-permute-done.5.refs_0_, bf16[64,3072]{1,0:T(8,128)(2,1)S(1)} %collective-permute-done.6.refs_1_, bf16[128,3072]{1,0:T(8,128)(2,1)S(1)} %collective-permute-done.7.refs_2_, bf16[128,3072]{1,0:T(8,128)(2,1)S(1)} %collective-permute-done.8.refs_3_, ...), custom_call_target="tpu_custom_call" | custom-call | flops 2717908992 | bytes 9437184 | tf_op jit(solution)/shard_map/project/pallas_call | solution.py:65
  133.7 3.7 %project.15.refs_7_ = bf16[3,128,384]{2,1,0:T(8,128)(2,1)S(1)} custom-call(bf16[64,3072]{1,0:T(8,128)(2,1)S(1)} %collective-permute-done.9.refs_0_, bf16[64,3072]{1,0:T(8,128)(2,1)S(1)} %collective-permute-done.10.refs_1_, f32[2,3072]{1,0:T(2,128)S(1)} %bitcast.41, bf16[3,3072,384]{2,1,0:T(8,128)(2,1)S(1)} %bitcast.29), custom_call_target="tpu_custom_call" | custom-call | flops 905969664 | bytes 7864320 | tf_op jit(solution)/shard_map/project/pallas_call | solution.py:65
  139.6 4.4 %copy.12.refs_8_ = bf16[384,3072]{1,0:T(8,128)(2,1)} copy(bf16[384,3072]{0,1:T(8,128)(2,1)} %all-gather.5.cloned.1.call-done) | data formatting | bytes 4718592 | tf_op jit(solution)/shard_map/all_gather | solution.py:171
  150.7 10.0 %project.10.refs_2_ = bf16[3,384,384]{2,1,0:T(8,128)(2,1)S(1)} custom-call(bf16[64,3072]{1,0:T(8,128)(2,1)S(1)} %collective-permute-done.5.refs_0_, bf16[64,3072]{1,0:T(8,128)(2,1)S(1)} %copy-done.8, bf16[128,3072]{1,0:T(8,128)(2,1)S(1)} %copy-done.4, bf16[128,3072]{1,0:T(8,128)(2,1)S(1)} %copy-done.6, f32[2,3072]{1,0:T(2,128)S(1)} %bitcast.35, ...), custom_call_target="tpu_custom_call" | custom-call | flops 2717908992 | bytes 9437184 | tf_op jit(solution)/shard_map/project/pallas_call | solution.py:65
  161.9 14.7 %project.9.refs_1_ = bf16[3,512,384]{2,1,0:T(8,128)(2,1)S(1)} custom-call(bf16[128,3072]{1,0:T(8,128)(2,1)} %constant_dynamic-update-slice_fusion.refs_0_, bf16[128,3072]{1,0:T(8,128)(2,1)S(1)} %copy-done.20, bf16[128,3072]{1,0:T(8,128)(2,1)S(1)} %copy-done.22, bf16[128,3072]{1,0:T(8,128)(2,1)} %collective-permute-done.4.refs_3_, f32[2,3072]{1,0:T(2,128)S(1)} %bitcast.36, ...), custom_call_target="tpu_custom_call" | custom-call | flops 3623878656 | bytes 10223616 | tf_op jit(solution)/shard_map/project/pallas_call | solution.py:65
  177.8 11.8 %project.8.refs_0_ = bf16[2,512,384]{2,1,0:T(8,128)(2,1)S(1)} custom-call(bf16[512,3072]{1,0:T(8,128)(2,1)S(1)} %bitcast.33, f32[2,3072]{1,0:T(2,128)S(1)} %bitcast.37, bf16[3,3072,384]{2,1,0:T(8,128)(2,1)S(1)} %bitcast.31), custom_call_target="tpu_custom_call" | custom-call | flops 2415919104 | bytes 7864320 | tf_op jit(solution)/shard_map/project/pallas_call | solution.py:65
  189.6 8.9 %attend.5 = (bf16[64,3072]{1,0:T(8,128)(2,1)S(1)}, bf16[64,3072]{1,0:T(8,128)(2,1)S(1)}, bf16[64,3072]{1,0:T(8,128)(2,1)S(1)}, bf16[64,3072]{1,0:T(8,128)(2,1)S(1)}) custom-call(bf16[2,512,384]{2,1,0:T(8,128)(2,1)S(1)} %project.8.refs_0_, bf16[3,512,384]{2,1,0:T(8,128)(2,1)} %copy-done.24, bf16[3,384,384]{2,1,0:T(8,128)(2,1)S(1)} %project.10.refs_2_, ...), custom_call_target="tpu_custom_call" | custom-call | flops 4831838208 | bytes 13369344 | tf_op jit(solution)/shard_map/attend/pallas_call | solution.py:139
  198.5 8.9 %attend.6 = (bf16[64,3072]{1,0:T(8,128)(2,1)S(1)}, bf16[64,3072]{1,0:T(8,128)(2,1)S(1)}, bf16[64,3072]{1,0:T(8,128)(2,1)S(1)}, bf16[64,3072]{1,0:T(8,128)(2,1)S(1)}) custom-call(bf16[2,512,384]{2,1,0:T(8,128)(2,1)S(1)} %project.8.refs_0_, bf16[3,512,384]{2,1,0:T(8,128)(2,1)} %copy-done.24, bf16[3,384,384]{2,1,0:T(8,128)(2,1)S(1)} %project.10.refs_2_, ...), custom_call_target="tpu_custom_call" | custom-call | flops 4831838208 | bytes 13369344 | tf_op jit(solution)/shard_map/attend/pallas_call | solution.py:139
  207.3 9.1 %attend.7 = (bf16[64,3072]{1,0:T(8,128)(2,1)S(1)}, bf16[64,3072]{1,0:T(8,128)(2,1)S(1)}, bf16[64,3072]{1,0:T(8,128)(2,1)S(1)}, bf16[64,3072]{1,0:T(8,128)(2,1)S(1)}) custom-call(bf16[2,512,384]{2,1,0:T(8,128)(2,1)S(1)} %project.8.refs_0_, bf16[3,512,384]{2,1,0:T(8,128)(2,1)} %copy-done.24, bf16[3,384,384]{2,1,0:T(8,128)(2,1)S(1)} %project.10.refs_2_, ...), custom_call_target="tpu_custom_call" | custom-call | flops 4831838208 | bytes 13369344 | tf_op jit(solution)/shard_map/attend/pallas_call | solution.py:139
  223.1 8.8 %attend.4 = (bf16[64,3072]{1,0:T(8,128)(2,1)S(1)}, bf16[64,3072]{1,0:T(8,128)(2,1)S(1)}, bf16[64,3072]{1,0:T(8,128)(2,1)S(1)}, bf16[64,3072]{1,0:T(8,128)(2,1)S(1)}) custom-call(bf16[2,512,384]{2,1,0:T(8,128)(2,1)S(1)} %project.8.refs_0_, bf16[3,512,384]{2,1,0:T(8,128)(2,1)} %copy-done.24, bf16[3,384,384]{2,1,0:T(8,128)(2,1)S(1)} %project.10.refs_2_, ...), custom_call_target="tpu_custom_call" | custom-call | flops 4831838208 | bytes 13369344 | tf_op jit(solution)/shard_map/attend/pallas_call | solution.py:139
  232.8 5.4 %collective-permute-done.15 = bf16[64,3072]{1,0:T(8,128)(2,1)S(1)} collective-permute-done((bf16[64,3072]{1,0:T(8,128)(2,1)S(1)}, bf16[64,3072]{1,0:T(8,128)(2,1)S(1)}, u32[]{:S(2)}, u32[]{:S(2)}) %collective-permute-start.15) | collective-permute-done | bytes 393248 | tf_op jit(solution)/shard_map/ppermute | solution.py:199
  239.9 7.5 %collective-permute-done.18 = bf16[64,3072]{1,0:T(8,128)(2,1)S(1)} collective-permute-done((bf16[64,3072]{1,0:T(8,128)(2,1)S(1)}, bf16[64,3072]{1,0:T(8,128)(2,1)S(1)}, u32[]{:S(2)}, u32[]{:S(2)}) %collective-permute-start.18) | collective-permute-done | bytes 393248 | tf_op jit(solution)/shard_map/ppermute | solution.py:199
  255.8 11.3 %collective-permute-done.16 = bf16[64,3072]{1,0:T(8,128)(2,1)S(1)} collective-permute-done((bf16[64,3072]{1,0:T(8,128)(2,1)S(1)}, bf16[64,3072]{1,0:T(8,128)(2,1)S(1)}, u32[]{:S(2)}, u32[]{:S(2)}) %collective-permute-start.16) | collective-permute-done | bytes 393248 | tf_op jit(solution)/shard_map/ppermute | solution.py:199
  269.4 8.6 %collective-permute-done.22 = bf16[64,3072]{1,0:T(8,128)(2,1)S(1)} collective-permute-done((bf16[64,3072]{1,0:T(8,128)(2,1)S(1)}, bf16[64,3072]{1,0:T(8,128)(2,1)S(1)}, u32[]{:S(2)}, u32[]{:S(2)}) %collective-permute-start.22) | collective-permute-done | bytes 393248 | tf_op jit(solution)/shard_map/ppermute | solution.py:199
  281.8 5.5 %collective-permute-done.17 = bf16[64,3072]{1,0:T(8,128)(2,1)S(1)} collective-permute-done((bf16[64,3072]{1,0:T(8,128)(2,1)S(1)}, bf16[64,3072]{1,0:T(8,128)(2,1)S(1)}, u32[]{:S(2)}, u32[]{:S(2)}) %collective-permute-start.17) | collective-permute-done | bytes 393248 | tf_op jit(solution)/shard_map/ppermute | solution.py:199
  287.5 4.0 %collective-permute-done.24 = bf16[64,3072]{1,0:T(8,128)(2,1)S(1)} collective-permute-done((bf16[64,3072]{1,0:T(8,128)(2,1)S(1)}, bf16[64,3072]{1,0:T(8,128)(2,1)S(1)}, u32[]{:S(2)}, u32[]{:S(2)}) %collective-permute-start.24) | collective-permute-done | bytes 393248 | tf_op jit(solution)/shard_map/ppermute | solution.py:199
  (133 shorter events, 59.0 us)
Async XLA Ops:
  6.5 133.1 %all-gather.5.cloned.1.call-start = ((), (), s32[]{:S(2)}) async-start(), calls=%async_computation.1 | async-start | bytes 2506752 | tf_op jit(solution)/shard_map/all_gather | solution.py:171
  7.3 136.7 %all-gather.3.cloned.1.call-start = ((), (), s32[]{:S(2)}) async-start(), calls=%async_computation | async-start | bytes 7520256 | tf_op jit(solution)/shard_map/all_gather | solution.py:170
  10.7 13.9 %collective-permute-start = (bf16[64,3072]{1,0:T(8,128)(2,1)S(1)}, bf16[64,3072]{1,0:T(8,128)(2,1)S(1)}, u32[]{:S(2)}, u32[]{:S(2)}) collective-permute-start(bf16[64,3072]{1,0:T(8,128)(2,1)S(1)} %get-tuple-element.40), channel_id=1, source_target_pairs={{0,0},{1,16},{2,32},{3,48},{4,64},{5,80},{6,96},{7,112},{8,8},{9,2... | collective-permute-start | bytes 1179656 | tf_op jit(solution)/shard_map/ppermute | solution.py:188
  13.1 17.6 %collective-permute-start.1 = (bf16[64,3072]{1,0:T(8,128)(2,1)S(1)}, bf16[64,3072]{1,0:T(8,128)(2,1)S(1)}, u32[]{:S(2)}, u32[]{:S(2)}) collective-permute-start(bf16[64,3072]{1,0:T(8,128)(2,1)S(1)} %get-tuple-element.39), channel_id=1, source_target_pairs={{0,8},{1,24},{2,40},{3,56},{4,72},{5,88},{6,104},{7,120},{8,0},{9,... | collective-permute-start | bytes 1179656 | tf_op jit(solution)/shard_map/ppermute | solution.py:189
  31.5 25.7 %collective-permute-start.4 = (bf16[128,3072]{1,0:T(8,128)(2,1)}, bf16[128,3072]{1,0:T(8,128)(2,1)}, u32[]{:S(2)}, u32[]{:S(2)}) collective-permute-start(bf16[128,3072]{1,0:T(8,128)(2,1)} %constant_dynamic-update-slice_fusion.refs_0_), channel_id=1, source_target_pairs={{0,1},{1,0},{2,3},{3,2},{4,5},{5,4},{6,7},{7,6},{8,9},{9,8},{10,11... | collective-permute-start | bytes 2359304 | tf_op jit(solution)/shard_map/ppermute | solution.py:199
  32.8 56.7 %collective-permute-start.2 = (bf16[128,3072]{1,0:T(8,128)(2,1)}, bf16[128,3072]{1,0:T(8,128)(2,1)S(1)}, u32[]{:S(2)}, u32[]{:S(2)}) collective-permute-start(bf16[128,3072]{1,0:T(8,128)(2,1)} %constant_dynamic-update-slice_fusion.refs_0_), channel_id=1, source_target_pairs={{0,2},{1,3},{2,4},{3,5},{4,6},{5,7},{6,0},{7,1},{8,10},{9,11},{10,... | collective-permute-start | bytes 2359304 | tf_op jit(solution)/shard_map/ppermute | solution.py:199
  52.4 37.3 %collective-permute-start.3 = (bf16[128,3072]{1,0:T(8,128)(2,1)}, bf16[128,3072]{1,0:T(8,128)(2,1)S(1)}, u32[]{:S(2)}, u32[]{:S(2)}) collective-permute-start(bf16[128,3072]{1,0:T(8,128)(2,1)} %constant_dynamic-update-slice_fusion.refs_0_), channel_id=1, source_target_pairs={{0,6},{1,7},{2,0},{3,1},{4,2},{5,3},{6,4},{7,5},{8,14},{9,15},{10,... | collective-permute-start | bytes 2359304 | tf_op jit(solution)/shard_map/ppermute | solution.py:199
  57.2 48.9 %collective-permute-start.7 = (bf16[128,3072]{1,0:T(8,128)(2,1)}, bf16[128,3072]{1,0:T(8,128)(2,1)S(1)}, u32[]{:S(2)}, u32[]{:S(2)}) collective-permute-start(bf16[128,3072]{1,0:T(8,128)(2,1)} %collective-permute-done.4.refs_3_), channel_id=1, source_target_pairs={{0,2},{1,3},{2,4},{3,5},{4,6},{5,7},{6,0},{7,1},{8,10},{9,11},{10,... | collective-permute-start | bytes 2359304 | tf_op jit(solution)/shard_map/ppermute | solution.py:199
  78.2 26.4 %collective-permute-start.8 = (bf16[128,3072]{1,0:T(8,128)(2,1)}, bf16[128,3072]{1,0:T(8,128)(2,1)S(1)}, u32[]{:S(2)}, u32[]{:S(2)}) collective-permute-start(bf16[128,3072]{1,0:T(8,128)(2,1)} %collective-permute-done.4.refs_3_), channel_id=1, source_target_pairs={{0,6},{1,7},{2,0},{3,1},{4,2},{5,3},{6,4},{7,5},{8,14},{9,15},{10,... | collective-permute-start | bytes 2359304 | tf_op jit(solution)/shard_map/ppermute | solution.py:199
  89.6 33.1 %collective-permute-start.5 = (bf16[64,3072]{1,0:T(8,128)(2,1)S(1)}, bf16[64,3072]{1,0:T(8,128)(2,1)S(1)}, u32[]{:S(2)}, u32[]{:S(2)}) collective-permute-start(bf16[64,3072]{1,0:T(8,128)(2,1)S(1)} %slice.28), channel_id=1, source_target_pairs={{0,2},{1,3},{2,4},{3,5},{4,6},{5,7},{6,0},{7,1},{8,10},{9,11},{10,... | collective-permute-start | bytes 1179656 | tf_op jit(solution)/shard_map/ppermute | solution.py:199
  89.7 33.0 %collective-permute-start.6 = (bf16[64,3072]{1,0:T(8,128)(2,1)S(1)}, bf16[64,3072]{1,0:T(8,128)(2,1)S(1)}, u32[]{:S(2)}, u32[]{:S(2)}) collective-permute-start(bf16[64,3072]{1,0:T(8,128)(2,1)S(1)} %slice.29), channel_id=1, source_target_pairs={{0,6},{1,7},{2,0},{3,1},{4,2},{5,3},{6,4},{7,5},{8,14},{9,15},{10,... | collective-permute-start | bytes 1179656 | tf_op jit(solution)/shard_map/ppermute | solution.py:199
  104.6 29.0 %collective-permute-start.10 = (bf16[64,3072]{1,0:T(8,128)(2,1)S(1)}, bf16[64,3072]{1,0:T(8,128)(2,1)S(1)}, u32[]{:S(2)}, u32[]{:S(2)}) collective-permute-start(bf16[64,3072]{1,0:T(8,128)(2,1)S(1)} %slice.31), channel_id=1, source_target_pairs={{0,6},{1,7},{2,0},{3,1},{4,2},{5,3},{6,4},{7,5},{8,14},{9,15},{10,... | collective-permute-start | bytes 1179656 | tf_op jit(solution)/shard_map/ppermute | solution.py:199
  106.1 27.6 %collective-permute-start.9 = (bf16[64,3072]{1,0:T(8,128)(2,1)S(1)}, bf16[64,3072]{1,0:T(8,128)(2,1)S(1)}, u32[]{:S(2)}, u32[]{:S(2)}) collective-permute-start(bf16[64,3072]{1,0:T(8,128)(2,1)S(1)} %slice.30), channel_id=1, source_target_pairs={{0,2},{1,3},{2,4},{3,5},{4,6},{5,7},{6,0},{7,1},{8,10},{9,11},{10,... | collective-permute-start | bytes 1179656 | tf_op jit(solution)/shard_map/ppermute | solution.py:199
  216.4 15.5 %collective-permute-start.12 = (bf16[64,3072]{1,0:T(8,128)(2,1)S(1)}, bf16[64,3072]{1,0:T(8,128)(2,1)S(1)}, u32[]{:S(2)}, u32[]{:S(2)}) collective-permute-start(bf16[64,3072]{1,0:T(8,128)(2,1)S(1)} %get-tuple-element.24), channel_id=1, source_target_pairs={{0,2},{1,3},{2,4},{3,5},{4,6},{5,7},{6,0},{7,1},{8,10},{9,11},{10,... | collective-permute-start | bytes 1179656 | tf_op jit(solution)/shard_map/ppermute | solution.py:199
  216.6 21.6 %collective-permute-start.15 = (bf16[64,3072]{1,0:T(8,128)(2,1)S(1)}, bf16[64,3072]{1,0:T(8,128)(2,1)S(1)}, u32[]{:S(2)}, u32[]{:S(2)}) collective-permute-start(bf16[64,3072]{1,0:T(8,128)(2,1)S(1)} %get-tuple-element.28), channel_id=1, source_target_pairs={{0,2},{1,3},{2,4},{3,5},{4,6},{5,7},{6,0},{7,1},{8,10},{9,11},{10,... | collective-permute-start | bytes 1179656 | tf_op jit(solution)/shard_map/ppermute | solution.py:199
  218.1 36.1 %collective-permute-start.14 = (bf16[64,3072]{1,0:T(8,128)(2,1)S(1)}, bf16[64,3072]{1,0:T(8,128)(2,1)S(1)}, u32[]{:S(2)}, u32[]{:S(2)}) collective-permute-start(bf16[64,3072]{1,0:T(8,128)(2,1)S(1)} %get-tuple-element.26), channel_id=1, source_target_pairs={{0,6},{1,7},{2,0},{3,1},{4,2},{5,3},{6,4},{7,5},{8,14},{9,15},{10,... | collective-permute-start | bytes 1179656 | tf_op jit(solution)/shard_map/ppermute | solution.py:199
  219.8 58.4 %collective-permute-start.11 = (bf16[64,3072]{1,0:T(8,128)(2,1)S(1)}, bf16[64,3072]{1,0:T(8,128)(2,1)S(1)}, u32[]{:S(2)}, u32[]{:S(2)}) collective-permute-start(bf16[64,3072]{1,0:T(8,128)(2,1)S(1)} %get-tuple-element.22), channel_id=1, source_target_pairs={{0,6},{1,7},{2,0},{3,1},{4,2},{5,3},{6,4},{7,5},{8,14},{9,15},{10,... | collective-permute-start | bytes 1179656 | tf_op jit(solution)/shard_map/ppermute | solution.py:199
  221.8 25.6 %collective-permute-start.18 = (bf16[64,3072]{1,0:T(8,128)(2,1)S(1)}, bf16[64,3072]{1,0:T(8,128)(2,1)S(1)}, u32[]{:S(2)}, u32[]{:S(2)}) collective-permute-start(bf16[64,3072]{1,0:T(8,128)(2,1)S(1)} %get-tuple-element.31), channel_id=1, source_target_pairs={{0,6},{1,7},{2,0},{3,1},{4,2},{5,3},{6,4},{7,5},{8,14},{9,15},{10,... | collective-permute-start | bytes 1179656 | tf_op jit(solution)/shard_map/ppermute | solution.py:199
  232.0 55.5 %collective-permute-start.20 = (bf16[64,3072]{1,0:T(8,128)(2,1)S(1)}, bf16[64,3072]{1,0:T(8,128)(2,1)S(1)}, u32[]{:S(2)}, u32[]{:S(2)}) collective-permute-start(bf16[64,3072]{1,0:T(8,128)(2,1)S(1)} %get-tuple-element.32), channel_id=1, source_target_pairs={{0,2},{1,3},{2,4},{3,5},{4,6},{5,7},{6,0},{7,1},{8,10},{9,11},{10,... | collective-permute-start | bytes 1179656 | tf_op jit(solution)/shard_map/ppermute | solution.py:199
  238.2 14.2 %collective-permute-start.21 = (bf16[64,3072]{1,0:T(8,128)(2,1)S(1)}, bf16[64,3072]{1,0:T(8,128)(2,1)S(1)}, u32[]{:S(2)}, u32[]{:S(2)}) collective-permute-start(bf16[64,3072]{1,0:T(8,128)(2,1)S(1)} %get-tuple-element.35), channel_id=1, source_target_pairs={{0,6},{1,7},{2,0},{3,1},{4,2},{5,3},{6,4},{7,5},{8,14},{9,15},{10,... | collective-permute-start | bytes 1179656 | tf_op jit(solution)/shard_map/ppermute | solution.py:199
  247.4 20.7 %collective-permute-start.23 = (bf16[64,3072]{1,0:T(8,128)(2,1)S(1)}, bf16[64,3072]{1,0:T(8,128)(2,1)S(1)}, u32[]{:S(2)}, u32[]{:S(2)}) collective-permute-start(bf16[64,3072]{1,0:T(8,128)(2,1)S(1)} %get-tuple-element.36), channel_id=1, source_target_pairs={{0,2},{1,3},{2,4},{3,5},{4,6},{5,7},{6,0},{7,1},{8,10},{9,11},{10,... | collective-permute-start | bytes 1179656 | tf_op jit(solution)/shard_map/ppermute | solution.py:199
  252.4 14.8 %collective-permute-start.16 = (bf16[64,3072]{1,0:T(8,128)(2,1)S(1)}, bf16[64,3072]{1,0:T(8,128)(2,1)S(1)}, u32[]{:S(2)}, u32[]{:S(2)}) collective-permute-start(bf16[64,3072]{1,0:T(8,128)(2,1)S(1)} %add_convert_fusion.7), channel_id=1, source_target_pairs={{0,2},{1,3},{2,4},{3,5},{4,6},{5,7},{6,0},{7,1},{8,10},{9,11},{10,... | collective-permute-start | bytes 1179656 | tf_op jit(solution)/shard_map/ppermute | solution.py:199
  254.2 27.6 %collective-permute-start.13 = (bf16[64,3072]{1,0:T(8,128)(2,1)S(1)}, bf16[64,3072]{1,0:T(8,128)(2,1)S(1)}, u32[]{:S(2)}, u32[]{:S(2)}) collective-permute-start(bf16[64,3072]{1,0:T(8,128)(2,1)S(1)} %add_convert_fusion.8), channel_id=1, source_target_pairs={{0,2},{1,3},{2,4},{3,5},{4,6},{5,7},{6,0},{7,1},{8,10},{9,11},{10,... | collective-permute-start | bytes 1179656 | tf_op jit(solution)/shard_map/ppermute | solution.py:199
  268.0 19.5 %collective-permute-start.19 = (bf16[64,3072]{1,0:T(8,128)(2,1)S(1)}, bf16[64,3072]{1,0:T(8,128)(2,1)S(1)}, u32[]{:S(2)}, u32[]{:S(2)}) collective-permute-start(bf16[64,3072]{1,0:T(8,128)(2,1)S(1)} %add_convert_fusion.4), channel_id=1, source_target_pairs={{0,6},{1,7},{2,0},{3,1},{4,2},{5,3},{6,4},{7,5},{8,14},{9,15},{10,... | collective-permute-start | bytes 1179656 | tf_op jit(solution)/shard_map/ppermute | solution.py:199
  (33 other events, 385.7 us)
Sparse Core Ops, SparseCore 0:
  9.1 64.6 all-gather.4
  75.4 48.8 all-gather.2
